TPU v7x, 256 devices: a whole 4x4x8 slice. The times are simulated.
256 devices in a mesh: row: 32 (over z_lo, y, x), col: 8 (over z_hi, core).
Axes of the slice: x: 4, y: 4, z: 8 (z_hi: 4, z_lo: 2; z = z_hi * 2 + z_lo), core: 2. Of those that a mesh axis runs over, the one named last changes fastest.
Arguments:
- latent: bfloat16 [12288, 512], P('row', 'col'), may hold values from -6 to 6
- w_kv: bfloat16 [512, 8192], P('row', 'col'), may hold values from -0.25 to 0.25
- queries: bfloat16 [12288, 4096], P('row', 'col'), may hold values from -240 to 240
- w_out: bfloat16 [4096, 7168], P('row', 'col'), may hold values from -0.09375 to 0.09375
Outputs:
- mixed: bfloat16 [12288, 7168], P('row', 'col')
All inputs are finite; a program needn't handle non-finite values.
Results may differ from a plain program's by a relative error of at most 0.012.
The roundings to bfloat16 on the way count: a program that leaves them out, or rounds other values in their place, can miss the bound.
Values may be sent and summed in bfloat16 or wider, within the bound.
A program may use at most 128 MiB of HBM per device.

v0:
```python
import math

import jax
import jax.numpy as jnp
from jax import lax
from jax.sharding import PartitionSpec as P

HEAD = 128


NEG_FILL = -1e30


def per_device(latent, w_kv, queries, w_out):
    row_count = lax.axis_size("row")
    tok_rows = latent.shape[0]
    per_col = queries.shape[1] // HEAD
    quarters = row_count // per_col
    stripe = tok_rows // quarters
    my_row = lax.axis_index("row")
    head_local = my_row % per_col
    quarter = my_row // per_col
    pair_width = 2 * HEAD
    latent_rows = lax.all_gather(latent, "col", axis=1, tiled=True)
    panel = lax.all_gather(w_kv, "row", axis=0, tiled=True)
    own_panel = lax.dynamic_slice_in_dim(panel, head_local * pair_width, pair_width, 1)
    keyvals = jnp.dot(
        lax.all_gather(latent_rows, "row", axis=0, tiled=True),
        own_panel,
        preferred_element_type=jnp.float32,
    ).astype(jnp.bfloat16)
    split_queries = queries.reshape(quarters, stripe, per_col, HEAD).transpose(0, 2, 1, 3)
    split_queries = split_queries.reshape(row_count, stripe, HEAD)
    my_queries = lax.all_to_all(
        split_queries, "row", split_axis=0, concat_axis=1, tiled=True
    ).reshape(row_count * stripe, HEAD)
    sources_per_block = row_count
    for candidate in range(1, row_count + 1):
        if row_count % candidate == 0 and candidate * stripe >= 256:
            sources_per_block = candidate
            break
    block_rows = sources_per_block * stripe
    key_span = sources_per_block * tok_rows
    key_block = math.gcd(key_span, 512)
    score_scale = HEAD ** (-0.5)
    pieces_done = []
    for block_index in range(row_count // sources_per_block):
        query_block = my_queries[block_index * block_rows : (block_index + 1) * block_rows]
        local_rows = jnp.arange(block_rows, dtype=jnp.int32)
        query_pos = (
            (block_index * sources_per_block + local_rows // stripe) * tok_rows
            + quarter * stripe
            + local_rows % stripe
        )

        def key_turn(key_index, carry, query_block=query_block, query_pos=query_pos):
            running_max, running_sum, weighted = carry
            first_key = key_index * key_block
            pairs = lax.dynamic_slice_in_dim(keyvals, first_key, key_block, 0)
            scores = (
                lax.dot_general(
                    query_block,
                    pairs[:, :HEAD],
                    (((1,), (1,)), ((), ())),
                    preferred_element_type=jnp.float32,
                )
                * score_scale
            )
            key_pos = first_key + jnp.arange(key_block, dtype=jnp.int32)
            allowed = key_pos[None, :] <= query_pos[:, None]
            scores = jnp.where(allowed, scores, NEG_FILL)
            new_max = jnp.maximum(running_max, jnp.max(scores, axis=1))
            rescale = jnp.exp(running_max - new_max)
            weights = jnp.where(allowed, jnp.exp(scores - new_max[:, None]), 0.0)
            running_sum = running_sum * rescale + jnp.sum(weights, axis=1)
            weighted = weighted * rescale[:, None] + jnp.dot(
                weights.astype(jnp.bfloat16), pairs[:, HEAD:], preferred_element_type=jnp.float32
            )
            return (new_max, running_sum, weighted)

        starting = (
            jnp.full((block_rows,), NEG_FILL, jnp.float32),
            jnp.zeros((block_rows,), jnp.float32),
            jnp.zeros((block_rows, HEAD), jnp.float32),
        )
        last_pos = (
            ((block_index + 1) * sources_per_block - 1) * tok_rows + quarter * stripe + stripe - 1
        )
        key_steps = (last_pos + key_block) // key_block
        final_max, final_sum, final_weighted = lax.fori_loop(0, key_steps, key_turn, starting)
        pieces_done.append((final_weighted / final_sum[:, None]).astype(jnp.bfloat16))
    attended = jnp.concatenate(pieces_done, axis=0)
    returned = lax.all_to_all(
        attended.reshape(row_count, stripe, HEAD), "row", split_axis=0, concat_axis=0, tiled=True
    )
    attn_tokens = (
        returned.reshape(quarters, per_col, stripe, HEAD)
        .transpose(0, 2, 1, 3)
        .reshape(tok_rows, per_col * HEAD)
    )
    full_features = lax.all_gather(attn_tokens, "col", axis=1, tiled=True)
    mixed = jnp.dot(
        full_features,
        lax.all_gather(w_out, "row", axis=0, tiled=True),
        preferred_element_type=jnp.float32,
    )
    return mixed.astype(jnp.bfloat16)


def solution(mesh):
    in_specs = (P("row", "col"), P("row", "col"), P("row", "col"), P("row", "col"))
    out_specs = P("row", "col")
    return jax.shard_map(
        per_device, mesh=mesh, in_specs=in_specs, out_specs=out_specs, check_vma=False
    )
```

profile of v0, /device:TPU:57, one launch (start us, length us, event | category | flops | bytes accessed | tf_op | source)
XLA Modules:
  0.0 610.9 jit_solution(13605765080693819022)
XLA Ops:
  7.3 19.3 %all_gather.16 = bf16[384,512]{0,1:T(8,128)(2,1)} all-gather(bf16[384,64]{0,1:T(8,128)(2,1)} %param.12), channel_id=1, replica_groups=mesh['row'=32,'col'=8] {'col'}, dimensions={1}, use_global_device_ids=true | all-gather | bytes 442368 | tf_op jit(solution)/shard_map/all_gather | solution.py:24
  28.5 7.7 %all-to-all-start = ((bf16[32,48,128]{2,1,0:T(8,128)(2,1)}), bf16[32,48,128]{2,1,0:T(8,128)(2,1)S(1)}, u32[]{:S(2)}, u32[]{:S(2)}) async-start(bf16[32,48,128]{2,1,0:T(8,128)(2,1)} %bitcast.2), calls=%async_computation | async-start | bytes 786432 | tf_op jit(solution)/shard_map/all_to_all | solution.py:34
  37.2 6.7 %all-to-all-done = bf16[32,48,128]{2,1,0:T(8,128)(2,1)S(1)} async-done(((bf16[32,48,128]{2,1,0:T(8,128)(2,1)}), bf16[32,48,128]{2,1,0:T(8,128)(2,1)S(1)}, u32[]{:S(2)}, u32[]{:S(2)}) %all-to-all-start) | async-done | bytes 393248 | tf_op jit(solution)/shard_map/all_to_all | solution.py:34
  43.9 94.1 %all-gather.5.cloned.1.call-done = bf16[512,1024]{1,0:T(8,128)(2,1)} async-done(((bf16[16,1024]{1,0:T(8,128)(2,1)}), bf16[512,1024]{1,0:T(8,128)(2,1)}) %all-gather.5.cloned.1.call-update) | async-done | bytes 1048592 | tf_op jit(solution)/shard_map/all_gather | solution.py:25
  138.0 188.4 %all-gather.7.cloned.1.call-done = bf16[12288,512]{0,1:T(8,128)(2,1)} async-done(((bf16[384,512]{0,1:T(8,128)(2,1)}), bf16[12288,512]{0,1:T(8,128)(2,1)}) %all-gather.7.cloned.1.call-update) | async-done | bytes 12582928 | tf_op jit(solution)/shard_map/all_gather | solution.py:28
  326.4 10.8 %fusion.103 = bf16[12288,256]{0,1:T(8,128)(2,1)} fusion(bf16[12288,512]{0,1:T(8,128)(2,1)} %all-gather.7.cloned.1.call-done, bf16[512,1024]{1,0:T(8,128)(2,1)} %all-gather.5.cloned.1.call-done, s32[]{:T(128)S(6)} %select_n.100), kind=kOutput, calls=%fused_computation.136 | convolution fusion | flops 3224371200 | bytes 19136516 | tf_op jit(solution)/shard_map/dot_general | solution.py:27
  337.2 8.6 %copy.16 = bf16[12288,256]{1,0:T(8,128)(2,1)} copy(bf16[12288,256]{0,1:T(8,128)(2,1)} %fusion.103) | data formatting | bytes 12582912
  345.9 17.2 %while.60 = (s32[]{:T(128)}, f32[384]{0:T(512)S(1)}, f32[384]{0:T(512)S(1)}, f32[384,128]{1,0:T(8,128)S(1)}, s32[]{:T(128)}, /*index=5*/bf16[12288,256]{1,0:T(8,...) while((s32[]{:T(128)}, f32[384]{0:T(512)S(1)}, ...), condition=%wide.region_3.4_spmd.clone, body=%wide.region_0.3_spmd.clone.sunk | while | flops 103127936 | bytes 3152075 | solution.py:90
  347.4 1.4 convolution_add_fusion.8
  350.2 1.4 convolution_add_fusion.8
  353.1 1.4 convolution_add_fusion.8
  356.0 1.4 convolution_add_fusion.8
  358.8 1.4 convolution_add_fusion.8
  361.7 1.4 convolution_add_fusion.8
  363.2 34.5 %while.61 = (s32[]{:T(128)}, f32[384]{0:T(512)S(1)}, f32[384]{0:T(512)S(1)}, f32[384,128]{1,0:T(8,128)S(1)}, s32[]{:T(128)}, /*index=5*/bf16[12288,256]{1,0:T(8,...) while((s32[]{:T(128)}, f32[384]{0:T(512)S(1)}, ...), condition=%wide.region_7.8_spmd.clone, body=%wide.region_4.7_spmd.clone.sunk | while | flops 103128320 | bytes 3152075 | solution.py:90
  364.6 1.4 convolution_add_fusion.9
  367.5 1.4 convolution_add_fusion.9
  370.4 1.4 convolution_add_fusion.9
  373.2 1.4 convolution_add_fusion.9
  376.1 1.4 convolution_add_fusion.9
  379.0 1.4 convolution_add_fusion.9
  381.9 1.4 convolution_add_fusion.9
  384.7 1.4 convolution_add_fusion.9
  387.6 1.4 convolution_add_fusion.9
  393.3 1.4 convolution_add_fusion.9
  396.2 1.4 convolution_add_fusion.9
  397.9 51.4 %while.62 = (s32[]{:T(128)}, f32[384]{0:T(512)S(1)}, f32[384]{0:T(512)S(1)}, f32[384,128]{1,0:T(8,128)S(1)}, s32[]{:T(128)}, /*index=5*/bf16[12288,256]{1,0:T(8,...) while((s32[]{:T(128)}, f32[384]{0:T(512)S(1)}, ...), condition=%wide.region_11.12_spmd.clone, body=%wide.region_8.11_spmd.clone.sunk | while | flops 103128320 | bytes 3152075 | solution.py:90
  449.4 68.7 %while.63 = (s32[]{:T(128)}, f32[384]{0:T(512)S(1)}, f32[384]{0:T(512)S(1)}, f32[384,128]{1,0:T(8,128)S(1)}, s32[]{:T(128)}, /*index=5*/bf16[12288,256]{1,0:T(8,...) while((s32[]{:T(128)}, f32[384]{0:T(512)S(1)}, ...), condition=%wide.region_15.16_spmd.clone, body=%wide.region_12.15_spmd.clone.sunk | while | flops 103128320 | bytes 3152075 | solution.py:90
  482.3 1.4 convolution_add_fusion.11
  518.3 17.0 %all_to_all.14 = bf16[32,48,128]{2,1,0:T(8,128)(2,1)S(1)} all-to-all(bf16[32,48,128]{2,1,0:T(8,128)(2,1)S(1)} %bitcast.49), channel_id=1, replica_groups=mesh['row'=32,'col'=8] {'row'}, dimensions={0} | all-to-all | bytes 786432 | tf_op jit(solution)/shard_map/all_to_all | solution.py:93
  536.3 59.7 %all-gather.9.cloned.1.call-done = bf16[384,4096]{1,0:T(8,128)(2,1)} async-done(((bf16[384,512]{1,0:T(8,128)(2,1)}), bf16[384,4096]{1,0:T(8,128)(2,1)}) %all-gather.9.cloned.1.call-update) | async-done | bytes 3145744 | tf_op jit(solution)/shard_map/all_gather | solution.py:101
  596.1 8.3 %convolution_convert_fusion.1 = bf16[384,896]{1,0:T(8,128)(2,1)} fusion(bf16[384,4096]{1,0:T(8,128)(2,1)} %all-gather.9.cloned.1.call-done, bf16[4096,896]{1,0:T(8,128)(2,1)} %all-gather.11.cloned.1.call-done), kind=kOutput, calls=%fused_computation.137 | convolution fusion | flops 2818916352 | bytes 11173888 | tf_op jit(solution)/shard_map/dot_general | solution.py:102
  (491 shorter events, 148.6 us)
Async XLA Ops:
  6.5 131.5 %all-gather.5.cloned.1.call-start = ((), (), s32[]{:S(2)}) async-start(), calls=%async_computation.2 | async-start | bytes 1081344 | tf_op jit(solution)/shard_map/all_gather | solution.py:25
  7.3 319.2 %all-gather.7.cloned.1.call-start = ((), (), s32[]{:S(2)}) async-start(), calls=%async_computation.3 | async-start | bytes 12976128 | tf_op jit(solution)/shard_map/all_gather | solution.py:28
  28.5 15.3 %all-to-all-start = ((bf16[32,48,128]{2,1,0:T(8,128)(2,1)}), bf16[32,48,128]{2,1,0:T(8,128)(2,1)S(1)}, u32[]{:S(2)}, u32[]{:S(2)}) async-start(bf16[32,48,128]{2,1,0:T(8,128)(2,1)} %bitcast.2), calls=%async_computation | async-start | bytes 786432 | tf_op jit(solution)/shard_map/all_to_all | solution.py:34
  36.3 500.1 %all-gather.11.cloned.1.call-start = ((), (), s32[]{:S(2)}) async-start(), calls=%async_computation.5 | async-start | bytes 7569408 | tf_op jit(solution)/shard_map/all_gather | solution.py:104
  37.0 559.1 %all-gather.9.cloned.1.call-start = ((), (), s32[]{:S(2)}) async-start(), calls=%async_computation.4 | async-start | bytes 3538944 | tf_op jit(solution)/shard_map/all_gather | solution.py:101
Sparse Core Ops, SparseCore 0:
  9.1 128.8 all-gather.4
  139.8 186.5 all-gather.6
  328.2 164.7 all-gather.10
  536.4 59.6 all-gather.8
where the time goes:
time: 618 us; the launch traced here: 611 us
  waiting for transfers between devices  350 us (57%)
  matrix products  174 us (28%)
  blocking collectives  36.3 us (6%)
  other arithmetic  14.2 us (2%)
  between operations  13.4 us (2%)
  local copies, waits for them, and re-layouts  11.7 us (2%)
  starting transfers between devices  7.84 us (1%)
    all_gather x1, waiting for transfers between devices, per_device(): lax.all_gather(latent_rows, 'row', axis=0, tiled=True)  188 us
    all_gather x1, waiting for transfers between devices, per_device(): panel = lax.all_gather(w_kv, 'row', axis=0, tiled=True)  94.1 us
    dot_general x60, matrix products, key_turn(): jnp.dot(weights.astype(jnp.bfloat16), pairs[:, HEAD:], preferred_element_...  82.7 us
    dot_general x60, matrix products, key_turn(): lax.dot_general(query_block, pairs[:, :HEAD], (((1,), (1,)), ((), ())), p...  71.9 us
    all_gather x1, waiting for transfers between devices, per_device(): full_features = lax.all_gather(attn_tokens, 'col', axis=1, tiled=True)  59.7 us
    all_gather x1, blocking collectives, per_device(): latent_rows = lax.all_gather(latent, 'col', axis=1, tiled=True)  19.3 us
    all_to_all x1, blocking collectives, per_device(): lax.all_to_all(attended.reshape(row_count, stripe, HEAD), 'row', split_ax...  17 us
  transfers between devices with their start and end apart: 5, of which 4 were waited for; matrix products, arithmetic and copies ran while one was open for 31% of the time, Pallas kernels for 0%

commit v1 on v0

v1 whole, which is shorter than its diff:
```python
import functools

import jax
import jax.numpy as jnp
from jax import lax
from jax.experimental import pallas as pl
from jax.experimental.pallas import tpu as pltpu
from jax.sharding import PartitionSpec as P

HEAD = 128
NEG_FILL = -1e30
MESH = pl.DeviceIdType.MESH
BF16 = jnp.bfloat16
F32 = jnp.float32

ROWS = 32
TOK = 384
STRIPE = 48
QROWS = 4
QB = QROWS * STRIPE
KB = QROWS * TOK
BLOCKS = ROWS // QROWS
SCALE = HEAD**-0.5 * 1.4426950408889634


def kernel(
    lat_ref, wkv_ref, q_ref, wout_ref, out_ref,
    pieces, lat, wkv, wkt, queries, keys_t, values, att, feats, wout, acc, top, total,
    cs, cr, qs, qr, ws, wr, gs, gr, ss, sr, os, orr, hs, hr, zs, zr, ls,
):
    row = lax.axis_index("row")
    col = lax.axis_index("col")
    x = lax.rem(row, 4)
    y = lax.rem(row // 4, 4)
    zl = row // 16
    zh = col // 2
    core = lax.rem(col, 2)
    sibling = (row, zh * 2 + 1 - core)

    def row_of(xx, yy, zz):
        return zz * 16 + yy * 4 + xx

    def up(v):
        return lax.rem(v + 1, 4)

    def down(v):
        return lax.rem(v + 3, 4)

    def across(v):
        return lax.rem(v + 2, 4)

    def remote(src, dst, send, recv, device):
        return pltpu.make_async_remote_copy(
            src_ref=src, dst_ref=dst, send_sem=send, recv_sem=recv,
            device_id=device, device_id_type=MESH,
        )

    barrier = pltpu.get_barrier_semaphore()

    def greet_row(d, carry):
        pl.semaphore_signal(
            barrier, inc=1, device_id=(lax.rem(row + d, ROWS), col), device_id_type=MESH
        )
        return carry

    def greet_col(d, carry):
        pl.semaphore_signal(
            barrier, inc=1, device_id=(row, lax.rem(col + d, 8)), device_id_type=MESH
        )
        return carry

    lax.fori_loop(1, 8, greet_col, 0)
    lax.fori_loop(1, ROWS, greet_row, 0)
    pl.semaphore_wait(barrier, ROWS - 1 + 7)

    home = zh // 2
    own_slot = lax.rem(zh, 2) * 2 + core

    def col_copy(d):
        dst = (row, lax.rem(zh + d, 4) * 2 + home)
        return remote(lat_ref, pieces.at[own_slot], cs.at[d], cr.at[own_slot], dst)

    for d in (2, 1, 3):
        col_copy(d).start()

    @pl.when(core != home)
    def _():
        col_copy(0).start()

    own_piece = pltpu.make_async_copy(lat_ref, pieces.at[own_slot], ls.at[0])

    @pl.when(core == home)
    def _():
        own_piece.start()

    head_local = x

    def q_copy(d):
        peer = lax.rem(row + d, ROWS)
        part = q_ref.at[
            pl.ds(pl.multiple_of(peer // 4 * STRIPE, STRIPE), STRIPE),
            pl.ds(pl.multiple_of(lax.rem(peer, 4) * HEAD, HEAD), HEAD),
        ]
        return part, remote(part, queries.at[row], qs.at[d], qr.at[d], (peer, col))

    def w_copy(d):
        peer = lax.rem(row + d, ROWS)
        part = wkv_ref.at[:, pl.ds(pl.multiple_of(lax.rem(peer, 4) * 256, 256), 256)]
        return part, remote(part, wkv.at[row], ws.at[d], wr.at[d], (peer, col))

    def small_start(d, carry):
        w_copy(d)[1].start()
        q_copy(d)[1].start()
        return carry

    lax.fori_loop(1, ROWS, small_start, 0)
    local_q = pltpu.make_async_copy(q_copy(0)[0], queries.at[row], ls.at[1])
    local_w = pltpu.make_async_copy(w_copy(0)[0], wkv.at[row], ls.at[2])
    local_q.start()
    local_w.start()

    def axes(half):
        if half == 0:
            return x, y, lambda aa, bb, zz: row_of(aa, bb, zz)
        return y, x, lambda aa, bb, zz: row_of(bb, aa, zz)

    def lat_copy(half, n):
        a, b, dev = axes(half)
        buf = lat.at[core * 2 + half]

        def at(aa, bb, zz, count):
            return buf.at[pl.ds((aa * 4 + bb) * 2 + zz, count)]

        if n == 0:
            src, to = at(a, b, zl, 1), dev(a, b, 1 - zl)
        elif n == 1:
            src, to = at(a, b, 0, 2), dev(a, up(b), zl)
        elif n == 2:
            src, to = at(a, b, 0, 2), dev(a, down(b), zl)
        elif n == 3:
            src, to = at(a, down(b), 0, 1), dev(a, up(b), zl)
        elif n == 4:
            src, to = at(a, up(b), 1, 1), dev(a, down(b), zl)
        elif n == 5:
            src, to = at(a, 0, 0, 8), dev(up(a), b, zl)
        elif n == 6:
            src, to = at(a, 0, 0, 8), dev(down(a), b, zl)
        elif n == 7:
            src, to = at(down(a), 0, 0, 4), dev(up(a), b, zl)
        else:
            src, to = at(up(a), 2, 0, 4), dev(down(a), b, zl)
        return remote(src, src, gs.at[half, n], gr.at[half, n], (to, col))

    def sib_copy(half, n):
        a, _, _ = axes(half)
        group = (a, down(a), up(a), across(a))[n]
        src = lat.at[core * 2 + half, pl.ds(group * 8, 8)]
        return remote(src, src, ss.at[half, n], sr.at[half, n], sibling)

    def out_copy(half, n):
        a, b, dev = axes(half)
        buf = wout.at[half]
        if n == 1 or n == 2:
            src = buf.at[a * 4 + b]
            to = dev(a, up(b) if n == 1 else down(b), zl)
        elif n == 3:
            src, to = buf.at[a * 4 + down(b), pl.ds(0, 64)], dev(a, up(b), zl)
        elif n == 4:
            src, to = buf.at[a * 4 + up(b), pl.ds(64, 64)], dev(a, down(b), zl)
        elif n == 5 or n == 6:
            src = buf.at[pl.ds(a * 4, 4)]
            to = dev(up(a) if n == 5 else down(a), b, zl)
        elif n == 7:
            src, to = buf.at[pl.ds(down(a) * 4, 2)], dev(up(a), b, zl)
        else:
            src, to = buf.at[pl.ds(up(a) * 4 + 2, 2)], dev(down(a), b, zl)
        return remote(src, src, os.at[half, n], orr.at[half, n], (to, col))

    own_out = wout.at[zl, jnp.where(zl == 0, x * 4 + y, y * 4 + x)]
    out_first = remote(wout_ref, own_out, os.at[0, 0], orr.at[0, 0], (row_of(x, y, 1 - zl), col))
    out_local = pltpu.make_async_copy(wout_ref, own_out, ls.at[3])

    @pl.when(core != home)
    def _():
        col_copy(0).wait_send()

    @pl.when(core == home)
    def _():
        own_piece.wait()

    def piece_arrival(slot):
        return remote(lat_ref, pieces.at[slot], cs.at[0], cr.at[slot], sibling)

    for slot in range(4):

        @pl.when(jnp.logical_not((core == home) & (own_slot == slot)))
        def _(slot=slot):
            piece_arrival(slot).wait_recv()

    for half in (0, 1):
        a, b, _ = axes(half)
        lat[core * 2 + half, (a * 4 + b) * 2 + zl] = jnp.concatenate(
            [pieces[half * 2], pieces[half * 2 + 1]], axis=1
        )
        lat_copy(half, 0).start()
    for half in (0, 1):
        lat_copy(half, 0).wait_recv()
        lat_copy(half, 1).start()
        lat_copy(half, 2).start()
    out_first.start()
    out_local.start()
    for half in (0, 1):
        lat_copy(half, 1).wait_recv()
        lat_copy(half, 3).start()
        lat_copy(half, 2).wait_recv()
        lat_copy(half, 4).start()
    for half in (0, 1):
        lat_copy(half, 3).wait_recv()
        lat_copy(half, 4).wait_recv()
        lat_copy(half, 5).start()
        lat_copy(half, 6).start()
        sib_copy(half, 0).start()

    def small_wait(d, carry):
        w_copy(d)[1].wait()
        q_copy(d)[1].wait()
        return carry

    lax.fori_loop(1, ROWS, small_wait, 0)
    local_q.wait()
    local_w.wait()
    wkt[...] = wkv[...].reshape(512, 256)[:, :HEAD].T
    values[:, HEAD:] = jnp.ones((ROWS * TOK, HEAD), BF16)

    for half in (0, 1):
        lat_copy(half, 5).wait_recv()
        lat_copy(half, 7).start()
        lat_copy(half, 6).wait_recv()
        lat_copy(half, 8).start()
        sib_copy(half, 1).start()
        sib_copy(half, 2).start()
    out_first.wait_recv()
    out_local.wait()
    for half in (0, 1):
        lat_copy(half, 7).wait_recv()
        lat_copy(half, 8).wait_recv()
        sib_copy(half, 3).start()
        out_copy(half, 1).start()
        out_copy(half, 2).start()
    for half in (0, 1):
        for n in range(4):
            sib_copy(half, n).wait_recv()

    def project(r, carry):
        xx = lax.rem(r, 4)
        yy = lax.rem(r // 4, 4)
        zz = r // 16
        first = (xx * 4 + yy) * 2 + zz
        second = (yy * 4 + xx) * 2 + zz
        tokens = jnp.concatenate(
            [lat[0, first], lat[1, second], lat[2, first], lat[3, second]], axis=1
        )
        at = pl.multiple_of(r * TOK, TOK)
        keys_t[:, pl.ds(at, TOK)] = lax.dot_general(
            wkt[...], tokens, (((1,), (1,)), ((), ())), preferred_element_type=F32
        ).astype(BF16)
        values[pl.ds(at, TOK), :HEAD] = jnp.dot(
            tokens, wkv[...].reshape(512, 256)[:, HEAD:], preferred_element_type=F32
        ).astype(BF16)
        return carry

    lax.fori_loop(0, ROWS, project, 0)

    def att_copy(r, d):
        dst = feats.at[
            col,
            pl.ds(pl.multiple_of(row // 4 * STRIPE, STRIPE), STRIPE),
            pl.ds(pl.multiple_of(head_local * HEAD, HEAD), HEAD),
        ]
        return dst, remote(att.at[r], dst, hs.at[d], hr.at[d], (r, col))

    def out_steps(block):
        @pl.when(block == 2)
        def _():
            for half in (0, 1):
                out_copy(half, 1).wait_recv()
                out_copy(half, 3).start()
                out_copy(half, 2).wait_recv()
                out_copy(half, 4).start()

        @pl.when(block == 3)
        def _():
            for half in (0, 1):
                out_copy(half, 3).wait_recv()
                out_copy(half, 4).wait_recv()
                out_copy(half, 5).start()
                out_copy(half, 6).start()

        @pl.when(block == 7)
        def _():
            for half in (0, 1):
                out_copy(half, 5).wait_recv()
                out_copy(half, 7).start()
                out_copy(half, 6).wait_recv()
                out_copy(half, 8).start()

    def turn(query, first_key, allowed):
        first_key = pl.multiple_of(first_key, KB)
        scores = jnp.dot(query, keys_t[:, pl.ds(first_key, KB)], preferred_element_type=F32)
        if allowed is not None:
            scores = jnp.where(allowed, scores, NEG_FILL)
        before = top[:, :1]
        now = jnp.maximum(before, jnp.max(scores, axis=1, keepdims=True))
        weights = jnp.exp2((scores - now) * SCALE).astype(BF16)
        rescale = jnp.exp2((before - now) * SCALE)
        acc[...] = acc[...] * rescale + jnp.dot(
            weights, values[pl.ds(first_key, KB), :], preferred_element_type=F32
        )
        top[...] = jnp.broadcast_to(now, top.shape)

    def attend(block, carry):
        out_steps(block)
        query = queries[pl.ds(block * QROWS, QROWS)].reshape(QB, HEAD)
        acc[...] = jnp.zeros_like(acc)
        top[...] = jnp.full(top.shape, NEG_FILL, F32)

        def full(step, inner):
            turn(query, step * KB, None)
            return inner

        lax.fori_loop(0, block, full, 0)
        place = lax.broadcasted_iota(jnp.int32, (QB, KB), 0)
        key = lax.broadcasted_iota(jnp.int32, (QB, KB), 1)
        source = (
            (place >= STRIPE).astype(jnp.int32)
            + (place >= 2 * STRIPE).astype(jnp.int32)
            + (place >= 3 * STRIPE).astype(jnp.int32)
        )
        position = source * (TOK - STRIPE) + place + row // 4 * STRIPE
        turn(query, block * KB, key <= position)
        done = (acc[:, :HEAD] / acc[:, HEAD:]).astype(BF16)
        att[pl.ds(block * QROWS, QROWS)] = done.reshape(QROWS, STRIPE, HEAD)
        for j in range(QROWS):
            r = block * QROWS + j

            @pl.when(r != row)
            def _(r=r):
                att_copy(r, lax.rem(row - r + ROWS, ROWS))[1].start()

        return carry

    lax.fori_loop(0, BLOCKS, attend, 0)

    local_att = pltpu.make_async_copy(att.at[row], att_copy(row, 0)[0], ls.at[4])
    local_att.start()

    def att_wait(d, carry):
        att_copy(row, d)[1].wait_recv()
        return carry

    lax.fori_loop(1, ROWS, att_wait, 0)
    local_att.wait()

    def place_of(h, k):
        return h * 2 + k

    def feat_copy(n):
        if n == 0:
            src, to = feats.at[col], place_of(up(zh), core)
        elif n == 1:
            src, to = feats.at[col], place_of(down(zh), core)
        elif n == 2:
            src, to = feats.at[col], place_of(zh, 1 - core)
        elif n == 3:
            src, to = feats.at[place_of(down(zh), core), pl.ds(0, 192)], place_of(up(zh), core)
        elif n == 4:
            src, to = feats.at[place_of(up(zh), core), pl.ds(192, 192)], place_of(down(zh), core)
        elif n == 5:
            src, to = feats.at[place_of(down(zh), core)], place_of(zh, 1 - core)
        elif n == 6:
            src, to = feats.at[place_of(up(zh), core)], place_of(zh, 1 - core)
        else:
            src, to = feats.at[place_of(across(zh), core)], place_of(zh, 1 - core)
        return remote(src, src, zs.at[n], zr.at[n], (row, to))

    for n in range(3):
        feat_copy(n).start()
    for half in (0, 1):
        out_copy(half, 7).wait_recv()
        out_copy(half, 8).wait_recv()

    def mix(c, first):
        low = c // 4
        within = lax.rem(c, 4)
        weights = []
        for j in range(4):
            weights.append(wout[low, jnp.where(low == 0, j * 4 + within, within * 4 + j)])
        product = jnp.dot(
            feats[c], jnp.concatenate(weights, axis=0), preferred_element_type=F32
        )
        if first:
            total[...] = product
        else:
            total[...] += product

    mix(col, True)
    feat_copy(0).wait_recv()
    feat_copy(3).start()
    feat_copy(5).start()
    feat_copy(1).wait_recv()
    feat_copy(4).start()
    feat_copy(6).start()
    feat_copy(2).wait_recv()

    def mix_some(n, carry):
        h = jnp.where(n == 0, zh, jnp.where(lax.rem(n, 2) == 1, down(zh), up(zh)))
        k = jnp.where((n == 1) | (n == 2), core, 1 - core)
        mix(place_of(h, k), False)
        return carry

    lax.fori_loop(0, 3, mix_some, 0)
    feat_copy(3).wait_recv()
    feat_copy(4).wait_recv()
    feat_copy(7).start()
    feat_copy(5).wait_recv()
    feat_copy(6).wait_recv()
    lax.fori_loop(3, 5, mix_some, 0)
    mix(place_of(across(zh), core), False)
    feat_copy(7).wait_recv()
    mix(place_of(across(zh), 1 - core), False)
    out_ref[...] = total[...].astype(BF16)

    for d in (1, 2, 3):
        col_copy(d).wait_send()
    for half in (0, 1):
        for n in range(9):
            lat_copy(half, n).wait_send()
        for n in range(4):
            sib_copy(half, n).wait_send()
        for n in range(1, 9):
            out_copy(half, n).wait_send()
    out_first.wait_send()

    def att_sent(d, carry):
        att_copy(lax.rem(row - d + ROWS, ROWS), d)[1].wait_send()
        return carry

    lax.fori_loop(1, ROWS, att_sent, 0)
    for n in range(8):
        feat_copy(n).wait_send()


def per_device(latent, w_kv, queries, w_out):
    dma = pltpu.SemaphoreType.DMA
    vmem = pltpu.VMEM
    return pl.pallas_call(
        kernel,
        out_shape=jax.ShapeDtypeStruct((TOK, w_out.shape[1]), BF16),
        in_specs=[pl.BlockSpec(memory_space=pltpu.VMEM)] * 4,
        out_specs=pl.BlockSpec(memory_space=pltpu.VMEM),
        scratch_shapes=[
            vmem((4, TOK, 64), BF16),
            vmem((4, ROWS, TOK, 128), BF16),
            vmem((ROWS, 16, 256), BF16),
            vmem((128, 512), BF16),
            vmem((ROWS, STRIPE, HEAD), BF16),
            vmem((HEAD, ROWS * TOK), BF16),
            vmem((ROWS * TOK, 256), BF16),
            vmem((ROWS, STRIPE, HEAD), BF16),
            vmem((8, TOK, 512), BF16),
            vmem((2, 16, 128, 896), BF16),
            vmem((QB, 256), F32),
            vmem((QB, 128), F32),
            vmem((TOK, 896), F32),
            dma((4,)), dma((4,)),
            dma((ROWS,)), dma((ROWS,)),
            dma((ROWS,)), dma((ROWS,)),
            dma((2, 9)), dma((2, 9)),
            dma((2, 4)), dma((2, 4)),
            dma((2, 9)), dma((2, 9)),
            dma((ROWS,)), dma((ROWS,)),
            dma((8,)), dma((8,)),
            dma((5,)),
        ],
        compiler_params=pltpu.CompilerParams(
            collective_id=0, has_side_effects=True, vmem_limit_bytes=60 * 1024 * 1024
        ),
        cost_estimate=pl.CostEstimate(
            flops=12_000_000_000, bytes_accessed=2_000_000, transcendentals=11_000_000
        ),
    )(latent, w_kv, queries, w_out)


def solution(mesh):
    spec = P("row", "col")
    return jax.shard_map(
        per_device, mesh=mesh, in_specs=(spec,) * 4, out_specs=spec, check_vma=False
    )
```

time: 618 us -> 166 us (0.27); the launches traced: 611 us -> 166 us
  waiting for transfers between devices: 350 us -> 0 us
  matrix products: 174 us -> 0 us
  Pallas kernels: 0 us -> 162 us
  blocking collectives: 36.3 us -> 0 us
  other arithmetic: 14.2 us -> 0 us
  between operations: 13.4 us -> 0.01 us
  local copies, waits for them, and re-layouts: 11.7 us -> 3.54 us
  starting transfers between devices: 7.84 us -> 0 us
    all_gather x4 -> x0, waiting for transfers between devices: 342 us -> none  [the longest x1 188 us: per_device(): lax.all_gather(latent_rows, 'row', axis=0, tiled=True)]
    dot_general x122 -> x0, matrix products: 174 us -> none  [the longest x60 82.7 us: key_turn(): jnp.dot(weights.astype(jnp.bfloat16), pairs[:, HEAD:], preferred_element_...]
    pallas_call x0 -> x1, Pallas kernels: none -> 162 us  [per_device(): pl.pallas_call(kernel, out_shape=jax.ShapeDtypeStruct((TOK, w_out.shape[1...]
    all_gather x1 -> x0, blocking collectives: 19.3 us -> none  [per_device(): latent_rows = lax.all_gather(latent, 'col', axis=1, tiled=True)]
    all_to_all x1 -> x0, blocking collectives: 17 us -> none  [per_device(): lax.all_to_all(attended.reshape(row_count, stripe, HEAD), 'row', split_ax...]
    reduce_sum x60 -> x0, other arithmetic: 11.5 us -> none  [key_turn(): running_sum = running_sum * rescale + jnp.sum(weights, axis=1)]
    all_to_all x1 -> x0, starting transfers between devices: 7.72 us -> none  [per_device(): lax.all_to_all(split_queries, 'row', split_axis=0, concat_axis=1, tiled=T...]
    all_to_all x1 -> x0, waiting for transfers between devices: 6.73 us -> none  [per_device(): lax.all_to_all(split_queries, 'row', split_axis=0, concat_axis=1, tiled=T...]
  transfers between devices with their start and end apart: 5 -> 0, of which waited for: 4 -> 0; matrix products, arithmetic and copies ran while one was open for 31% -> 0% of each run, Pallas kernels for 0% -> 0%
where the time goes in v1:
time: 166 us
  Pallas kernels  162 us (98%)
  local copies, waits for them, and re-layouts  3.54 us (2%)
    pallas_call x1, Pallas kernels, per_device(): pl.pallas_call(kernel, out_shape=jax.ShapeDtypeStruct((TOK, w_out.shape[1...  162 us
    unnamed x2, local copies, waits for them, and re-layouts  3.54 us

profile of v1, /device:TPU:57, one launch (start us, length us, event | category | flops | bytes accessed | tf_op | source)
XLA Modules:
  0.0 165.9 jit_solution(15104496730388620658)
XLA Ops:
  0.0 1.5 copy.5.lat_ref
  1.5 162.3 %shard_map.46 = bf16[384,896]{1,0:T(8,128)(2,1)} custom-call(bf16[384,64]{1,0:T(8,128)(2,1)} %copy.5.lat_ref, bf16[16,1024]{1,0:T(8,128)(2,1)} %wkv_ref.1, bf16[384,512]{1,0:T(8,128)(2,1)} %q_ref.1, bf16[128,896]{1,0:T(8,128)(2,1)} %wout_ref.1), custom_call_target="tpu_custom_call" | custom-call | flops 12000000000 | bytes 2000000 | tf_op jit(solution)/shard_map/pallas_call | solution.py:456
  163.9 2.0 %copy.7 = bf16[384,896]{1,0:T(8,128)(2,1)} copy(bf16[384,896]{1,0:T(8,128)(2,1)} %shard_map.46) | data formatting | bytes 1376256

commit v2 on v1

v2 whole, which is shorter than its diff:
```python
import functools

import jax
import jax.numpy as jnp
from jax import lax
from jax.experimental import pallas as pl
from jax.experimental.pallas import tpu as pltpu
from jax.sharding import PartitionSpec as P

HEAD = 128
NEG_FILL = -1e30
MESH = pl.DeviceIdType.MESH
BF16 = jnp.bfloat16
F32 = jnp.float32

ROWS = 32
TOK = 384
STRIPE = 48
QROWS = 8
DIAG = 4
QB = QROWS * STRIPE
KB = QROWS * TOK
BLOCKS = ROWS // QROWS
SCALE = HEAD**-0.5 * 1.4426950408889634


def kernel(
    lat_ref, wkv_ref, q_ref, wout_ref, out_ref,
    lat, wkv, wkt, queries, keys_t, values, att, feats, wout, acc, top, total,
    cs, cr, qs, qr, ws, wr, gs, gr, ss, sr, os, orr, hs, hr, zs, zr, ls,
):
    row = lax.axis_index("row")
    col = lax.axis_index("col")
    x = lax.rem(row, 4)
    y = lax.rem(row // 4, 4)
    zl = row // 16
    zh = col // 2
    core = lax.rem(col, 2)
    sibling = (row, zh * 2 + 1 - core)

    def row_of(xx, yy, zz):
        return zz * 16 + yy * 4 + xx

    def up(v):
        return lax.rem(v + 1, 4)

    def down(v):
        return lax.rem(v + 3, 4)

    def across(v):
        return lax.rem(v + 2, 4)

    def remote(src, dst, send, recv, device):
        return pltpu.make_async_remote_copy(
            src_ref=src, dst_ref=dst, send_sem=send, recv_sem=recv,
            device_id=device, device_id_type=MESH,
        )

    barrier = pltpu.get_barrier_semaphore()

    def greet_row(d, carry):
        pl.semaphore_signal(
            barrier, inc=1, device_id=(lax.rem(row + d, ROWS), col), device_id_type=MESH
        )
        return carry

    def greet_col(d, carry):
        pl.semaphore_signal(
            barrier, inc=1, device_id=(row, lax.rem(col + d, 8)), device_id_type=MESH
        )
        return carry

    lax.fori_loop(1, 8, greet_col, 0)
    lax.fori_loop(1, ROWS, greet_row, 0)
    pl.semaphore_wait(barrier, ROWS - 1 + 7)

    home = zh // 2
    own_slot = lax.rem(zh, 2) * 2 + core
    slots = ((x * 4 + y) * 2 + zl, (y * 4 + x) * 2 + zl)
    own_place = lat.at[
        zh,
        jnp.where(lax.rem(zh, 2) == 0, slots[0], slots[1]),
        pl.ds(pl.multiple_of(core * 64, 64), 64),
    ]

    def col_copy(d):
        dst = (row, lax.rem(zh + d, 4) * 2 + home)
        return remote(lat_ref, own_place, cs.at[d], cr.at[own_slot], dst)

    for d in (2, 1, 3):
        col_copy(d).start()

    @pl.when(core != home)
    def _():
        col_copy(0).start()

    own_piece = pltpu.make_async_copy(lat_ref, own_place, ls.at[0])

    @pl.when(core == home)
    def _():
        own_piece.start()

    head_local = x

    def q_part(peer):
        return q_ref.at[
            pl.ds(pl.multiple_of(peer // 4 * STRIPE, STRIPE), STRIPE),
            pl.ds(pl.multiple_of(lax.rem(peer, 4) * HEAD, HEAD), HEAD),
        ]

    def w_part(peer):
        return wkv_ref.at[:, pl.ds(pl.multiple_of(lax.rem(peer, 4) * 256, 256), 256)]

    def q_copy(d):
        peer = lax.rem(row + d, ROWS)
        return remote(q_part(peer), queries.at[row], qs.at[d], qr.at[d], (peer, col))

    def w_copy(d):
        peer = lax.rem(row + d, ROWS)
        return remote(w_part(peer), wkv.at[row], ws.at[d], wr.at[d], (peer, col))

    def small_start(d, carry):
        w_copy(d).start()
        q_copy(d).start()
        return carry

    def axes(half):
        if half == 0:
            return x, y, lambda aa, bb, zz: row_of(aa, bb, zz)
        return y, x, lambda aa, bb, zz: row_of(bb, aa, zz)

    def lat_copy(half, n):
        a, b, dev = axes(half)
        buf = lat.at[core * 2 + half]
        across_b = (b, down(b), up(b), across(b))

        def at(aa, bb, zz, count):
            return buf.at[pl.ds((aa * 4 + bb) * 2 + zz, count)]

        if n == 0:
            src, to = at(a, b, zl, 1), dev(a, b, 1 - zl)
        elif n <= 4:
            src = at(a, b, zl if n <= 2 else 1 - zl, 1)
            to = dev(a, up(b) if n % 2 == 1 else down(b), zl)
        elif n == 5:
            src, to = at(a, down(b), zl, 1), dev(a, up(b), zl)
        elif n == 6:
            src, to = at(a, up(b), 1 - zl, 1), dev(a, down(b), zl)
        elif n < 11:
            src, to = at(a, across_b[n - 7], 0, 2), dev(up(a), b, zl)
        elif n < 15:
            src, to = at(a, across_b[n - 11], 0, 2), dev(down(a), b, zl)
        elif n < 19:
            src, to = at(down(a), across_b[n - 15], 0, 1), dev(up(a), b, zl)
        else:
            src, to = at(up(a), across_b[n - 19], 1, 1), dev(down(a), b, zl)
        return remote(src, src, gs.at[half, n], gr.at[half, n], (to, col))

    def sib_copy(half, g, j):
        a, b, _ = axes(half)
        aa = (a, down(a), up(a), across(a))[g]
        bb = (b, down(b), up(b), across(b))[j]
        src = lat.at[core * 2 + half, pl.ds((aa * 4 + bb) * 2, 2)]
        return remote(src, src, ss.at[half, g * 4 + j], sr.at[half, g * 4 + j], sibling)

    def out_copy(half, n):
        a, b, dev = axes(half)
        buf = wout.at[half]
        across_b = (b, down(b), up(b), across(b))
        if n <= 2:
            src = buf.at[a * 4 + b]
            to = dev(a, up(b) if n == 1 else down(b), zl)
        elif n == 3:
            src, to = buf.at[a * 4 + down(b), pl.ds(0, 64)], dev(a, up(b), zl)
        elif n == 4:
            src, to = buf.at[a * 4 + up(b), pl.ds(64, 64)], dev(a, down(b), zl)
        elif n < 9:
            src, to = buf.at[a * 4 + across_b[n - 5]], dev(up(a), b, zl)
        elif n < 13:
            src, to = buf.at[a * 4 + across_b[n - 9]], dev(down(a), b, zl)
        elif n < 17:
            src, to = buf.at[down(a) * 4 + across_b[n - 13], pl.ds(0, 64)], dev(up(a), b, zl)
        else:
            src, to = buf.at[up(a) * 4 + across_b[n - 17], pl.ds(64, 64)], dev(down(a), b, zl)
        return remote(src, src, os.at[half, n], orr.at[half, n], (to, col))

    own_out = wout.at[zl, jnp.where(zl == 0, x * 4 + y, y * 4 + x)]
    out_first = remote(wout_ref, own_out, os.at[0, 0], orr.at[0, 0], (row_of(x, y, 1 - zl), col))
    out_local = pltpu.make_async_copy(wout_ref, own_out, ls.at[3])

    out_local.start()
    out_local.wait()
    for half in (0, 1):

        @pl.when(zl == half)
        def _(half=half):
            for n in (1, 2, 5, 9):
                out_copy(half, n).start()

    @pl.when(core != home)
    def _():
        col_copy(0).wait_send()

    @pl.when(core == home)
    def _():
        own_piece.wait()

    def piece_arrival(slot):
        return remote(lat_ref, own_place, cs.at[0], cr.at[slot], sibling)

    for slot in range(4):

        @pl.when(jnp.logical_not((core == home) & (own_slot == slot)))
        def _(slot=slot):
            piece_arrival(slot).wait_recv()

    for half in (0, 1):
        for n in (0, 1, 2):
            lat_copy(half, n).start()
    lax.fori_loop(1, ROWS, small_start, 0)
    local_q = pltpu.make_async_copy(q_part(row), queries.at[row], ls.at[1])
    local_w = pltpu.make_async_copy(w_part(row), wkv.at[row], ls.at[2])
    local_q.start()
    local_w.start()
    for half in (0, 1):
        lat_copy(half, 0).wait_recv()
        for n in (3, 4, 7, 11):
            lat_copy(half, n).start()
        sib_copy(half, 0, 0).start()
    out_first.start()
    for half in (0, 1):
        lat_copy(half, 1).wait_recv()
        lat_copy(half, 5).start()
        lat_copy(half, 4).wait_recv()
        lat_copy(half, 6).start()
    for half in (0, 1):
        lat_copy(half, 3).wait_recv()
        for n in (8, 12):
            lat_copy(half, n).start()
        sib_copy(half, 0, 1).start()
        lat_copy(half, 2).wait_recv()
        for n in (9, 13):
            lat_copy(half, n).start()
        sib_copy(half, 0, 2).start()
    for half in (0, 1):
        lat_copy(half, 5).wait_recv()
        lat_copy(half, 6).wait_recv()
        for n in (10, 14):
            lat_copy(half, n).start()
        sib_copy(half, 0, 3).start()

    def small_wait(d, carry):
        w_copy(d).wait()
        q_copy(d).wait()
        return carry

    lax.fori_loop(1, ROWS, small_wait, 0)
    local_q.wait()
    local_w.wait()
    wkt[...] = wkv[...].reshape(512, 256).T
    values[:, HEAD:] = jnp.ones((ROWS * TOK, HEAD), BF16)

    for j in range(4):
        for half in (0, 1):
            lat_copy(half, 7 + j).wait_recv()
            lat_copy(half, 15 + j).start()
            sib_copy(half, 1, j).start()
            lat_copy(half, 11 + j).wait_recv()
            lat_copy(half, 19 + j).start()
            sib_copy(half, 2, j).start()
    for half in (0, 1):
        for g in range(3):
            for j in range(4):
                sib_copy(half, g, j).wait_recv()

    def project(i, carry):
        later = i - 9
        xx = jnp.where(i < 9, x + lax.rem(i, 3) + 3, jnp.where(later < 4, x + 2, x + later - 1))
        yy = jnp.where(i < 9, y + i // 3 + 3, jnp.where(later < 4, y + later, y + 2))
        xx = lax.rem(xx, 4)
        yy = lax.rem(yy, 4)
        for zz in (0, 1):
            first = (xx * 4 + yy) * 2 + zz
            second = (yy * 4 + xx) * 2 + zz
            tokens = jnp.concatenate(
                [lat[0, first], lat[1, second], lat[2, first], lat[3, second]], axis=0
            )
            at = pl.multiple_of(row_of(xx, yy, zz) * TOK, TOK)
            pair = jnp.dot(wkt[...], tokens, preferred_element_type=F32)
            keys_t[:, pl.ds(at, TOK)] = pair[:HEAD].astype(BF16)
            values[pl.ds(at, TOK), :HEAD] = pair[HEAD:].T.astype(BF16)
        return carry

    def last_group(j):
        for half in (0, 1):
            lat_copy(half, 15 + j).wait_recv()
            lat_copy(half, 19 + j).wait_recv()
            sib_copy(half, 3, j).start()

    lax.fori_loop(0, 3, project, 0)
    last_group(0)
    lax.fori_loop(3, 6, project, 0)
    last_group(1)
    out_first.wait_recv()
    for half in (0, 1):
        @pl.when(zl != half)
        def _(half=half):
            for n in (1, 2, 5, 9):
                out_copy(half, n).start()
    lax.fori_loop(6, 9, project, 0)
    last_group(2)
    last_group(3)
    for half in (0, 1):
        for j in range(4):
            sib_copy(half, 3, j).wait_recv()
    lax.fori_loop(9, 16, project, 0)

    att_place = feats.at[
        col,
        pl.ds(pl.multiple_of(row // 4 * STRIPE, STRIPE), STRIPE),
        pl.ds(pl.multiple_of(head_local * HEAD, HEAD), HEAD),
    ]

    def att_copy(r, d):
        return remote(att.at[r], att_place, hs.at[d], hr.at[d], (r, col))

    local_att = pltpu.make_async_copy(att.at[row], att_place, ls.at[4])

    def place_of(h, k):
        return h * 2 + k

    def feat_copy(n, part):
        lanes = pl.ds(pl.multiple_of(part * 256, 256), 256)

        def at(place, first, count):
            return feats.at[place, pl.ds(first, count), lanes]

        if n == 0:
            src, to = at(col, 0, TOK), place_of(up(zh), core)
        elif n == 1:
            src, to = at(col, 0, TOK), place_of(down(zh), core)
        elif n == 2:
            src, to = at(col, 0, TOK), place_of(zh, 1 - core)
        elif n == 3:
            src, to = at(place_of(down(zh), core), 0, 192), place_of(up(zh), core)
        elif n == 4:
            src, to = at(place_of(up(zh), core), 192, 192), place_of(down(zh), core)
        elif n == 5:
            src, to = at(place_of(down(zh), core), 0, TOK), place_of(zh, 1 - core)
        elif n == 6:
            src, to = at(place_of(up(zh), core), 0, TOK), place_of(zh, 1 - core)
        else:
            src, to = at(place_of(across(zh), core), 0, TOK), place_of(zh, 1 - core)
        return remote(src, src, zs.at[part, n], zr.at[part, n], (row, to))

    def feat_start(part):
        @pl.when(head_local // 2 == part)
        def _():
            local_att.start()

        def arrival(j, carry):
            source = j // 2 * 4 + part * 2 + lax.rem(j, 2)

            @pl.when(source != row)
            def _():
                att_copy(row, lax.rem(source - row + ROWS, ROWS)).wait_recv()

            return carry

        lax.fori_loop(0, ROWS // 2, arrival, 0)

        @pl.when(head_local // 2 == part)
        def _():
            local_att.wait()

        for n in range(3):
            feat_copy(n, part).start()

    def feat_forward(part):
        feat_copy(0, part).wait_recv()
        feat_copy(3, part).start()
        feat_copy(5, part).start()
        feat_copy(1, part).wait_recv()
        feat_copy(4, part).start()
        feat_copy(6, part).start()

    def feat_hand_over(part):
        feat_copy(3, part).wait_recv()
        feat_copy(4, part).wait_recv()
        feat_copy(7, part).start()

    turned = head_local // 2
    my_block = row // QROWS
    early = jnp.where(my_block == 3, 1, 0)

    def beside(tick):
        @pl.when(tick == 0)
        def _():
            for half in (0, 1):
                out_copy(half, 1).wait_recv()
                for n in (3, 6, 10):
                    out_copy(half, n).start()
                out_copy(half, 2).wait_recv()
                for n in (4, 7, 11):
                    out_copy(half, n).start()

        @pl.when(tick == 1)
        def _():
            for half in (0, 1):
                for n in (3, 4):
                    out_copy(half, n).wait_recv()
                for n in (8, 12):
                    out_copy(half, n).start()
                out_copy(half, 5).wait_recv()
                out_copy(half, 13).start()
                out_copy(half, 9).wait_recv()
                out_copy(half, 17).start()

        @pl.when(
            ((tick == 2) & (my_block == 0))
            | ((tick == 3) & (my_block == 1))
            | ((tick == 4) & (my_block == 3))
            | ((tick == 5) & (my_block == 2))
        )
        def _():
            feat_start(early)

        @pl.when(((tick == 4) & (my_block == 0)) | ((tick == 5) & (my_block == 1)))
        def _():
            feat_start(1 - early)

        @pl.when(tick == 3)
        def _():
            for half in (0, 1):
                out_copy(half, 6).wait_recv()
                out_copy(half, 14).start()
                out_copy(half, 10).wait_recv()
                out_copy(half, 18).start()

        @pl.when(tick == 5)
        def _():
            for half in (0, 1):
                out_copy(half, 7).wait_recv()
                out_copy(half, 15).start()
                out_copy(half, 11).wait_recv()
                out_copy(half, 19).start()

    def turn(query, start, first_key, keys, allowed):
        scores = jnp.dot(
            query[start:], keys_t[:, pl.ds(first_key, keys)], preferred_element_type=F32
        )
        if allowed is not None:
            scores = jnp.where(allowed, scores, NEG_FILL)
        before = top[start:, :1]
        now = jnp.maximum(before, jnp.max(scores, axis=1, keepdims=True))
        weights = jnp.exp2((scores - now) * SCALE).astype(BF16)
        rescale = jnp.exp2((before - now) * SCALE)
        acc[start:, :] = acc[start:, :] * rescale + jnp.dot(
            weights, values[pl.ds(first_key, keys), :], preferred_element_type=F32
        )
        top[start:, :] = jnp.broadcast_to(now, (QB - start, HEAD))

    def attend(turn_index, carry):
        block = lax.rem(turn_index + 3 * turned, BLOCKS)
        before = jnp.where(
            turned == 0,
            turn_index * (turn_index - 1) // 2,
            jnp.where(turn_index >= 2, turn_index + 1, 0),
        )
        query = queries[pl.ds(block * QROWS, QROWS)].reshape(QB, HEAD)
        acc[...] = jnp.zeros_like(acc)
        top[...] = jnp.full(top.shape, NEG_FILL, F32)

        def full(step, inner):
            beside(before + step)
            turn(query, 0, pl.multiple_of(step * KB, KB), KB, None)
            return inner

        lax.fori_loop(0, block, full, 0)
        for part in range(QROWS // DIAG):
            start = part * DIAG * STRIPE
            shape = (QB - start, DIAG * TOK)
            place = lax.broadcasted_iota(jnp.int32, shape, 0)
            key = lax.broadcasted_iota(jnp.int32, shape, 1)
            source = sum(
                (place >= STRIPE * j).astype(jnp.int32) for j in range(1, QROWS - part * DIAG)
            )
            position = source * (TOK - STRIPE) + place + row // 4 * STRIPE
            first_key = pl.multiple_of(block * KB + part * DIAG * TOK, DIAG * TOK)
            turn(query, start, first_key, DIAG * TOK, key <= position)
        done = (acc[:, :HEAD] / acc[:, HEAD:]).astype(BF16)
        att[pl.ds(block * QROWS, QROWS)] = done.reshape(QROWS, STRIPE, HEAD)
        for j in range(QROWS):
            r = block * QROWS + j

            @pl.when(r != row)
            def _(r=r):
                att_copy(r, lax.rem(row - r + ROWS, ROWS)).start()

        return carry

    lax.fori_loop(0, BLOCKS, attend, 0)

    for half in (0, 1):
        out_copy(half, 8).wait_recv()
        out_copy(half, 16).start()
        out_copy(half, 12).wait_recv()
        out_copy(half, 20).start()

    @pl.when(my_block >= 2)
    def _():
        feat_start(1 - early)

    feat_forward(early)

    feat_forward(1 - early)
    feat_hand_over(early)
    for half in (0, 1):
        for n in range(13, 21):
            out_copy(half, n).wait_recv()

    def mix(c, part, first=False):
        low = c // 4
        within = lax.rem(c, 4)
        weights = []
        for j in (0, 1):
            xx = part * 2 + j
            weights.append(wout[low, jnp.where(low == 0, xx * 4 + within, within * 4 + xx)])
        heads = feats[c, :, pl.ds(pl.multiple_of(part * 256, 256), 256)]
        product = jnp.dot(heads, jnp.concatenate(weights, axis=0), preferred_element_type=F32)
        if first:
            total[...] = product
        else:
            total[...] += product

    def mix_some(n, part):
        h = jnp.where(n == 0, zh, jnp.where(lax.rem(n, 2) == 1, down(zh), up(zh)))
        k = jnp.where((n == 1) | (n == 2), core, 1 - core)
        mix(place_of(h, k), part)
        return part

    mix(col, early, True)
    for part in (early, 1 - early):
        if part is not early:
            mix(col, part)
        feat_copy(2, part).wait_recv()
        lax.fori_loop(0, 3, mix_some, part)
        feat_copy(5, part).wait_recv()
        feat_copy(6, part).wait_recv()
        lax.fori_loop(3, 5, mix_some, part)
        if part is not early:
            feat_hand_over(part)
        mix(place_of(across(zh), core), part)
        feat_copy(7, part).wait_recv()
        mix(place_of(across(zh), 1 - core), part)
    out_ref[...] = total[...].astype(BF16)

    for d in (1, 2, 3):
        col_copy(d).wait_send()
    for half in (0, 1):
        for n in range(23):
            lat_copy(half, n).wait_send()
        for g in range(4):
            for j in range(4):
                sib_copy(half, g, j).wait_send()
        for n in range(1, 21):
            out_copy(half, n).wait_send()
    out_first.wait_send()

    def att_sent(d, carry):
        att_copy(lax.rem(row - d + ROWS, ROWS), d).wait_send()
        return carry

    lax.fori_loop(1, ROWS, att_sent, 0)
    for part in (0, 1):
        for n in range(8):
            feat_copy(n, part).wait_send()


def per_device(latent, w_kv, queries, w_out):
    dma = pltpu.SemaphoreType.DMA
    vmem = pltpu.VMEM
    return pl.pallas_call(
        kernel,
        out_shape=jax.ShapeDtypeStruct((TOK, w_out.shape[1]), BF16),
        in_specs=[pl.BlockSpec(memory_space=pltpu.VMEM)] * 4,
        out_specs=pl.BlockSpec(memory_space=pltpu.VMEM),
        scratch_shapes=[
            vmem((4, ROWS, 128, TOK), BF16),
            vmem((ROWS, 16, 256), BF16),
            vmem((256, 512), BF16),
            vmem((ROWS, STRIPE, HEAD), BF16),
            vmem((HEAD, ROWS * TOK), BF16),
            vmem((ROWS * TOK, 256), BF16),
            vmem((ROWS, STRIPE, HEAD), BF16),
            vmem((8, TOK, 512), BF16),
            vmem((2, 16, 128, 896), BF16),
            vmem((QB, 256), F32),
            vmem((QB, 128), F32),
            vmem((TOK, 896), F32),
            dma((4,)), dma((4,)),
            dma((ROWS,)), dma((ROWS,)),
            dma((ROWS,)), dma((ROWS,)),
            dma((2, 23)), dma((2, 23)),
            dma((2, 16)), dma((2, 16)),
            dma((2, 21)), dma((2, 21)),
            dma((ROWS,)), dma((ROWS,)),
            dma((2, 8)), dma((2, 8)),
            dma((5,)),
        ],
        compiler_params=pltpu.CompilerParams(
            collective_id=0, has_side_effects=True, vmem_limit_bytes=60 * 1024 * 1024
        ),
        cost_estimate=pl.CostEstimate(
            flops=12_000_000_000, bytes_accessed=2_000_000, transcendentals=11_000_000
        ),
    )(latent.T, w_kv, queries, w_out)


def solution(mesh):
    spec = P("row", "col")
    return jax.shard_map(
        per_device, mesh=mesh, in_specs=(spec,) * 4, out_specs=spec, check_vma=False
    )
```

time: 166 us -> 136 us (0.82)
  Pallas kernels: 162 us -> 133 us
    pallas_call x1, Pallas kernels: 162 us -> 133 us  [per_device(): pl.pallas_call(kernel, out_shape=jax.ShapeDtypeStruct((TOK, w_out.shape[1...]
    unnamed x2 -> x1, local copies, waits for them, and re-layouts: 3.54 us -> 2 us
where the time goes in v2:
time: 136 us; the launch traced here: 135 us
  Pallas kernels  133 us (98%)
  local copies, waits for them, and re-layouts  2 us (1%)
    pallas_call x1, Pallas kernels, per_device(): pl.pallas_call(kernel, out_shape=jax.ShapeDtypeStruct((TOK, w_out.shape[1...  133 us

profile of v2, /device:TPU:57, one launch (start us, length us, event | category | flops | bytes accessed | tf_op | source)
XLA Modules:
  0.0 135.5 jit_solution(2504658468021818961)
XLA Ops:
  0.0 133.5 %shard_map.46 = bf16[384,896]{1,0:T(8,128)(2,1)} custom-call(bf16[64,384]{1,0:T(8,128)(2,1)} %bitcast.1, bf16[16,1024]{1,0:T(8,128)(2,1)} %wkv_ref.1, bf16[384,512]{1,0:T(8,128)(2,1)} %q_ref.1, bf16[128,896]{1,0:T(8,128)(2,1)} %wout_ref.1), custom_call_target="tpu_custom_call" | custom-call | flops 12000000000 | bytes 2000000 | tf_op jit(solution)/shard_map/pallas_call | solution.py:583
  133.5 2.0 %copy.6 = bf16[384,896]{1,0:T(8,128)(2,1)} copy(bf16[384,896]{1,0:T(8,128)(2,1)} %shard_map.46) | data formatting | bytes 1376256

commit v3 on v2

--- a/solution.py
+++ b/solution.py
@@ -184,44 +184,76 @@
             src, to = buf.at[up(a) * 4 + across_b[n - 17], pl.ds(64, 64)], dev(down(a), b, zl)
         return remote(src, src, os.at[half, n], orr.at[half, n], (to, col))
 
+    def out_step(half, landed, sent):
+        for n in landed:
+            out_copy(half, n).wait_recv()
+        for n in sent:
+            out_copy(half, n).start()
+
+    first_steps = {
+        0: [((1,), (3, 6, 10)), ((2,), (4, 7, 11)), ((5,), (13,)), ((9,), (17,))],
+        1: [((3, 4), (8, 12)), ((6,), (14,)), ((10,), (18,))],
+        2: [((7,), (15,)), ((11,), (19,))],
+        3: [((8,), (16,)), ((12,), (20,))],
+    }
+    second_steps = {
+        0: [((), (1, 2, 5, 9))],
+        1: [((1,), (3, 6, 10)), ((2,), (4, 7, 11))],
+        2: [((5,), (13,)), ((9,), (17,))],
+        3: [((3, 4), (8, 12)), ((6,), (14,)), ((10,), (18,))],
+        4: [((7,), (15,)), ((11,), (19,))],
+        5: [((8,), (16,)), ((12,), (20,))],
+    }
+
+    def out_stage(stage):
+        if stage == 0:
+            out_first.wait_recv()
+        for steps, own in ((second_steps, False), (first_steps, True)):
+            for half in (0, 1):
+
+                @pl.when((zl == half) if own else (zl != half))
+                def _(half=half, steps=steps):
+                    for landed, sent in steps.get(stage, []):
+                        out_step(half, landed, sent)
+
     own_out = wout.at[zl, jnp.where(zl == 0, x * 4 + y, y * 4 + x)]
     out_first = remote(wout_ref, own_out, os.at[0, 0], orr.at[0, 0], (row_of(x, y, 1 - zl), col))
     out_local = pltpu.make_async_copy(wout_ref, own_out, ls.at[3])
 
-    out_local.start()
-    out_local.wait()
-    for half in (0, 1):
-
-        @pl.when(zl == half)
-        def _(half=half):
-            for n in (1, 2, 5, 9):
-                out_copy(half, n).start()
-
-    @pl.when(core != home)
-    def _():
-        col_copy(0).wait_send()
-
-    @pl.when(core == home)
-    def _():
-        own_piece.wait()
-
-    def piece_arrival(slot):
-        return remote(lat_ref, own_place, cs.at[0], cr.at[slot], sibling)
-
-    for slot in range(4):
-
-        @pl.when(jnp.logical_not((core == home) & (own_slot == slot)))
-        def _(slot=slot):
-            piece_arrival(slot).wait_recv()
-
-    for half in (0, 1):
-        for n in (0, 1, 2):
-            lat_copy(half, n).start()
     lax.fori_loop(1, ROWS, small_start, 0)
     local_q = pltpu.make_async_copy(q_part(row), queries.at[row], ls.at[1])
     local_w = pltpu.make_async_copy(w_part(row), wkv.at[row], ls.at[2])
     local_q.start()
     local_w.start()
+    out_local.start()
+    out_local.wait()
+    for half in (0, 1):
+
+        @pl.when(zl == half)
+        def _(half=half):
+            for n in (1, 2, 5, 9):
+                out_copy(half, n).start()
+
+    @pl.when(core != home)
+    def _():
+        col_copy(0).wait_send()
+
+    @pl.when(core == home)
+    def _():
+        own_piece.wait()
+
+    def piece_arrival(slot):
+        return remote(lat_ref, own_place, cs.at[0], cr.at[slot], sibling)
+
+    for slot in range(4):
+
+        @pl.when(jnp.logical_not((core == home) & (own_slot == slot)))
+        def _(slot=slot):
+            piece_arrival(slot).wait_recv()
+
+    for half in (0, 1):
+        for n in (0, 1, 2):
+            lat_copy(half, n).start()
     for half in (0, 1):
         lat_copy(half, 0).wait_recv()
         for n in (3, 4, 7, 11):
@@ -275,8 +307,11 @@
 
     def project(i, carry):
         later = i - 9
-        xx = jnp.where(i < 9, x + lax.rem(i, 3) + 3, jnp.where(later < 4, x + 2, x + later - 1))
-        yy = jnp.where(i < 9, y + i // 3 + 3, jnp.where(later < 4, y + later, y + 2))
+        j = later // 2
+        beyond = jnp.where(j == 0, 0, jnp.where(j == 1, 3, jnp.where(j == 2, 1, 2)))
+        even = lax.rem(later + 10, 2) == 0
+        xx = jnp.where(i < 9, x + lax.rem(i, 3) + 3, jnp.where(even, x + 2, x + beyond))
+        yy = jnp.where(i < 9, y + i // 3 + 3, jnp.where(even, y + beyond, y + 2))
         xx = lax.rem(xx, 4)
         yy = lax.rem(yy, 4)
         for zz in (0, 1):
@@ -301,19 +336,23 @@
     last_group(0)
     lax.fori_loop(3, 6, project, 0)
     last_group(1)
-    out_first.wait_recv()
-    for half in (0, 1):
-        @pl.when(zl != half)
-        def _(half=half):
-            for n in (1, 2, 5, 9):
-                out_copy(half, n).start()
+    out_stage(0)
     lax.fori_loop(6, 9, project, 0)
+
+    def last_handed(j):
+        for half in (0, 1):
+            sib_copy(half, 3, j).wait_recv()
+
+    last_handed(0)
+    lax.fori_loop(9, 11, project, 0)
     last_group(2)
+    last_handed(1)
+    lax.fori_loop(11, 13, project, 0)
     last_group(3)
-    for half in (0, 1):
-        for j in range(4):
-            sib_copy(half, 3, j).wait_recv()
-    lax.fori_loop(9, 16, project, 0)
+    last_handed(2)
+    lax.fori_loop(13, 15, project, 0)
+    last_handed(3)
+    project(15, 0)
 
     att_place = feats.at[
         col,
@@ -394,27 +433,11 @@
     early = jnp.where(my_block == 3, 1, 0)
 
     def beside(tick):
-        @pl.when(tick == 0)
-        def _():
-            for half in (0, 1):
-                out_copy(half, 1).wait_recv()
-                for n in (3, 6, 10):
-                    out_copy(half, n).start()
-                out_copy(half, 2).wait_recv()
-                for n in (4, 7, 11):
-                    out_copy(half, n).start()
-
-        @pl.when(tick == 1)
-        def _():
-            for half in (0, 1):
-                for n in (3, 4):
-                    out_copy(half, n).wait_recv()
-                for n in (8, 12):
-                    out_copy(half, n).start()
-                out_copy(half, 5).wait_recv()
-                out_copy(half, 13).start()
-                out_copy(half, 9).wait_recv()
-                out_copy(half, 17).start()
+        for after in range(1, 5):
+
+            @pl.when(tick == after + 1)
+            def _(after=after):
+                out_stage(after)
 
         @pl.when(
             ((tick == 2) & (my_block == 0))
@@ -428,22 +451,6 @@
         @pl.when(((tick == 4) & (my_block == 0)) | ((tick == 5) & (my_block == 1)))
         def _():
             feat_start(1 - early)
-
-        @pl.when(tick == 3)
-        def _():
-            for half in (0, 1):
-                out_copy(half, 6).wait_recv()
-                out_copy(half, 14).start()
-                out_copy(half, 10).wait_recv()
-                out_copy(half, 18).start()
-
-        @pl.when(tick == 5)
-        def _():
-            for half in (0, 1):
-                out_copy(half, 7).wait_recv()
-                out_copy(half, 15).start()
-                out_copy(half, 11).wait_recv()
-                out_copy(half, 19).start()
 
     def turn(query, start, first_key, keys, allowed):
         scores = jnp.dot(
@@ -501,15 +508,11 @@
 
     lax.fori_loop(0, BLOCKS, attend, 0)
 
-    for half in (0, 1):
-        out_copy(half, 8).wait_recv()
-        out_copy(half, 16).start()
-        out_copy(half, 12).wait_recv()
-        out_copy(half, 20).start()
-
     @pl.when(my_block >= 2)
     def _():
         feat_start(1 - early)
+
+    out_stage(5)
 
     feat_forward(early)
 

time: 136 us -> 130 us (0.956)
  Pallas kernels: 133 us -> 128 us
    pallas_call x1, Pallas kernels: 133 us -> 128 us  [per_device(): pl.pallas_call(kernel, out_shape=jax.ShapeDtypeStruct((TOK, w_out.shape[1...]
where the time goes in v3:
time: 130 us
  Pallas kernels  128 us (98%)
  local copies, waits for them, and re-layouts  2 us (2%)
    pallas_call x1, Pallas kernels, per_device(): pl.pallas_call(kernel, out_shape=jax.ShapeDtypeStruct((TOK, w_out.shape[1...  128 us

profile of v3, /device:TPU:57, one launch (start us, length us, event | category | flops | bytes accessed | tf_op | source)
XLA Modules:
  0.0 130.0 jit_solution(1667921838209720321)
XLA Ops:
  0.0 128.0 %shard_map.46 = bf16[384,896]{1,0:T(8,128)(2,1)} custom-call(bf16[64,384]{1,0:T(8,128)(2,1)} %bitcast.1, bf16[16,1024]{1,0:T(8,128)(2,1)} %wkv_ref.1, bf16[384,512]{1,0:T(8,128)(2,1)} %q_ref.1, bf16[128,896]{1,0:T(8,128)(2,1)} %wout_ref.1), custom_call_target="tpu_custom_call" | custom-call | flops 12000000000 | bytes 2000000 | tf_op jit(solution)/shard_map/pallas_call | solution.py:586
  128.0 2.0 %copy.6 = bf16[384,896]{1,0:T(8,128)(2,1)} copy(bf16[384,896]{1,0:T(8,128)(2,1)} %shard_map.46) | data formatting | bytes 1376256

commit v4 on v3

--- a/solution.py
+++ b/solution.py
@@ -443,10 +443,14 @@
             ((tick == 2) & (my_block == 0))
             | ((tick == 3) & (my_block == 1))
             | ((tick == 4) & (my_block == 3))
-            | ((tick == 5) & (my_block == 2))
+            | ((tick == 4) & (my_block == 2))
         )
         def _():
             feat_start(early)
+
+        @pl.when((tick == 5) & (my_block == 0))
+        def _():
+            feat_forward(early)
 
         @pl.when(((tick == 4) & (my_block == 0)) | ((tick == 5) & (my_block == 1)))
         def _():
@@ -514,7 +518,9 @@
 
     out_stage(5)
 
-    feat_forward(early)
+    @pl.when(my_block != 0)
+    def _():
+        feat_forward(early)
 
     feat_forward(1 - early)
     feat_hand_over(early)

time: 130 us -> 130 us (level)
  no operation moved by 1% of the time
where the time goes in v4:
time: 130 us
  Pallas kernels  128 us (98%)
  local copies, waits for them, and re-layouts  2 us (2%)
    pallas_call x1, Pallas kernels, per_device(): pl.pallas_call(kernel, out_shape=jax.ShapeDtypeStruct((TOK, w_out.shape[1...  128 us

profile of v4, /device:TPU:57, one launch (start us, length us, event | category | flops | bytes accessed | tf_op | source)
XLA Modules:
  0.0 129.6 jit_solution(3766434621336833875)
XLA Ops:
  0.0 127.6 %shard_map.46 = bf16[384,896]{1,0:T(8,128)(2,1)} custom-call(bf16[64,384]{1,0:T(8,128)(2,1)} %bitcast.1, bf16[16,1024]{1,0:T(8,128)(2,1)} %wkv_ref.1, bf16[384,512]{1,0:T(8,128)(2,1)} %q_ref.1, bf16[128,896]{1,0:T(8,128)(2,1)} %wout_ref.1), custom_call_target="tpu_custom_call" | custom-call | flops 12000000000 | bytes 2000000 | tf_op jit(solution)/shard_map/pallas_call | solution.py:592
  127.6 2.0 %copy.6 = bf16[384,896]{1,0:T(8,128)(2,1)} copy(bf16[384,896]{1,0:T(8,128)(2,1)} %shard_map.46) | data formatting | bytes 1376256

commit v5 on v4

--- a/solution.py
+++ b/solution.py
@@ -418,9 +418,9 @@
     def feat_forward(part):
         feat_copy(0, part).wait_recv()
         feat_copy(3, part).start()
-        feat_copy(5, part).start()
         feat_copy(1, part).wait_recv()
         feat_copy(4, part).start()
+        feat_copy(5, part).start()
         feat_copy(6, part).start()
 
     def feat_hand_over(part):

time: 130 us -> 130 us (level)
  no operation moved by 1% of the time
where the time goes in v5:
time: 130 us
  Pallas kernels  128 us (98%)
  local copies, waits for them, and re-layouts  2 us (2%)
    pallas_call x1, Pallas kernels, per_device(): pl.pallas_call(kernel, out_shape=jax.ShapeDtypeStruct((TOK, w_out.shape[1...  128 us

profile of v5, /device:TPU:57, one launch (start us, length us, event | category | flops | bytes accessed | tf_op | source)
XLA Modules:
  0.0 129.6 jit_solution(6941870839587114415)
XLA Ops:
  0.0 127.6 %shard_map.46 = bf16[384,896]{1,0:T(8,128)(2,1)} custom-call(bf16[64,384]{1,0:T(8,128)(2,1)} %bitcast.1, bf16[16,1024]{1,0:T(8,128)(2,1)} %wkv_ref.1, bf16[384,512]{1,0:T(8,128)(2,1)} %q_ref.1, bf16[128,896]{1,0:T(8,128)(2,1)} %wout_ref.1), custom_call_target="tpu_custom_call" | custom-call | flops 12000000000 | bytes 2000000 | tf_op jit(solution)/shard_map/pallas_call | solution.py:592
  127.6 2.0 %copy.6 = bf16[384,896]{1,0:T(8,128)(2,1)} copy(bf16[384,896]{1,0:T(8,128)(2,1)} %shard_map.46) | data formatting | bytes 1376256
